TPU v7x, 512 devices: a whole 4x8x8 slice. The times are simulated.
512 devices in a mesh: ctx: 128 (over y, z, core), head: 4 (over x).
Axes of the slice: x: 4, y: 8, z: 8, core: 2. Of those that a mesh axis runs over, the one named last changes fastest.
Arguments:
- queries: bfloat16 [2, 16384, 8192], P(None, ('ctx', 'head')), may hold values from -25 to 25
- keys: bfloat16 [2, 16384, 1024], P(None, ('ctx', 'head')), may hold values from -5.5 to 5.5
- values: bfloat16 [2, 16384, 1024], P(None, ('ctx', 'head')), may hold values from -6 to 6
- doc_lengths: int32 [47], replicated, may hold values from 1 to 1408, 32768 in all
Outputs:
- attended: bfloat16 [2, 16384, 8192], P(None, ('ctx', 'head'))
All inputs are finite; a program needn't handle non-finite values.
Results may differ from a plain program's by a relative error of at most 0.0045.
Values may be sent and summed in bfloat16 or wider, within the bound.
A program may use at most 64 MiB of HBM per device.

v0:
```python
import math
import jax
import jax.numpy as jnp
from jax import lax
from jax.sharding import PartitionSpec as P

HD = 128
REACH = 11
NEG_FILL = -1e30


def partner(block, axis, distance):
    count = lax.axis_size(axis)
    route = []
    for low in range(count):
        high = low | 1 << distance
        if high != low and high < count:
            route += [(low, high), (high, low)]
    return lax.ppermute(block, axis, route)


def shifted(block, axis, distance):
    devices = range(lax.axis_size(axis))
    route = [(i - distance, i) for i in devices if i - distance in devices]
    return lax.ppermute(block, axis, route)


def doc_of(positions, ends):
    return jnp.sum((positions[:, None] >= ends[None, :]).astype(jnp.int32), axis=1)


def attend(query, query_pos, keys, values, key_pos, ends, head_dim):
    rows = query.shape[0]
    kv_count = keys.shape[1] // head_dim
    group = query.shape[1] // head_dim // kv_count
    stride = min(group, 4)
    scale = 1.0 / math.sqrt(head_dim)
    allowed = (
        (doc_of(query_pos, ends)[:, None] == doc_of(key_pos, ends)[None, :])
        & (key_pos[None, :] <= query_pos[:, None])
        & (key_pos[None, :] >= 0)
    )
    pieces = []
    for kv_head in range(kv_count):
        key_head = keys[:, kv_head * head_dim : (kv_head + 1) * head_dim]
        value_head = values[:, kv_head * head_dim : (kv_head + 1) * head_dim]
        for portion in range(group // stride):
            first = (kv_head * group + portion * stride) * head_dim
            query_part = query[:, first : first + stride * head_dim].reshape(rows, stride, head_dim)
            scores = (
                jnp.einsum("rhd,sd->hrs", query_part, key_head, preferred_element_type=jnp.float32)
                * scale
            )
            masked = jnp.where(allowed[None], scores, NEG_FILL)
            top = jnp.max(masked, axis=2, keepdims=True)
            weights = jnp.where(allowed[None], jnp.exp(masked - top), 0.0)
            total = jnp.sum(weights, axis=2)
            mixed = jnp.einsum(
                "hrs,sd->rhd",
                weights.astype(jnp.bfloat16),
                value_head,
                preferred_element_type=jnp.float32,
            )
            pieces.append((mixed / total.T[:, :, None]).reshape(rows, stride * head_dim))
    return jnp.concatenate(pieces, axis=1).astype(jnp.bfloat16)


def half_attention(query, query_start, blocks, ends, head_dim):
    rows = query.shape[0]
    count = blocks.shape[0]
    width = blocks.shape[2] // 2
    query_pos = query_start + jnp.arange(rows, dtype=jnp.int32)
    window = blocks.reshape(count * rows, 2 * width)
    key_pos = query_start - (count - 1) * rows + jnp.arange(count * rows, dtype=jnp.int32)
    return attend(query, query_pos, window[:, :width], window[:, width:], key_pos, ends, head_dim)


def per_device(queries, keys, values, doc_lengths):
    head_dim = HD
    ctx_count = lax.axis_size("ctx")
    ctx_pos = lax.axis_index("ctx")
    reach = min(REACH, ctx_count // 2)
    query_local, key_local, value_local = (
        lax.all_to_all(queries, "head", split_axis=2, concat_axis=1, tiled=True),
        lax.all_to_all(keys, "head", split_axis=2, concat_axis=1, tiled=True),
        lax.all_to_all(values, "head", split_axis=2, concat_axis=1, tiled=True),
    )
    keyval = jnp.concatenate([key_local, value_local], axis=2)
    ends = jnp.cumsum(doc_lengths)
    rows = query_local.shape[1]
    query_width = query_local.shape[2]
    moving = jnp.concatenate([query_local[1], keyval[1]], axis=1)
    for digit in range(ctx_count.bit_length() - 1):
        moving = partner(moving, "ctx", digit)
    query_upper = moving[:, :query_width]
    keyval_upper = moving[:, query_width:]
    keyval_lower = keyval[0]
    held_pair = jnp.stack([keyval_lower, keyval_upper])
    earlier = []
    later = []
    for distance in range(1, reach + 1):
        earlier.append(shifted(keyval_lower, "ctx", distance))
        later.append(shifted(held_pair, "ctx", -distance))
    lower_blocks = jnp.stack(
        [earlier[distance - 1] for distance in range(reach, 0, -1)] + [keyval_lower]
    )
    lower_source = jnp.stack(
        [earlier[-offset - 1] for offset in range(-reach, 0)]
        + [keyval_lower]
        + [later[offset - 1][0] for offset in range(1, reach + 1)]
    )
    upper_source = jnp.stack(
        [keyval_upper] + [later[offset - 1][1] for offset in range(1, reach + 1)]
    )
    back_steps = jnp.arange(reach, -1, -1, dtype=jnp.int32)
    upper_index = 2 * ctx_count - 1 - ctx_pos
    target = upper_index - back_steps
    from_upper = target >= ctx_count
    offsets = jnp.clip(target - ctx_pos + reach, 0, 2 * reach)
    upper_blocks = jnp.where(
        from_upper[:, None, None],
        jnp.take(upper_source, back_steps, axis=0),
        jnp.take(lower_source, offsets, axis=0),
    )
    lower_out = half_attention(query_local[0], ctx_pos * rows, lower_blocks, ends, head_dim)
    upper_out = half_attention(query_upper, upper_index * rows, upper_blocks, ends, head_dim)
    for digit in range(ctx_count.bit_length() - 1):
        upper_out = partner(upper_out, "ctx", digit)
    result = jnp.stack([lower_out, upper_out])
    return lax.all_to_all(result, "head", split_axis=1, concat_axis=2, tiled=True)


def solution(mesh):
    placed = (
        P(None, ("ctx", "head"), None),
        P(None, ("ctx", "head"), None),
        P(None, ("ctx", "head"), None),
        P(),
    )
    return jax.shard_map(
        per_device,
        mesh=mesh,
        in_specs=placed,
        out_specs=P(None, ("ctx", "head"), None),
        check_vma=False,
    )
```

profile of v0, /device:TPU:248, one launch (start us, length us, event | category | flops | bytes accessed | tf_op | source)
XLA Modules:
  0.0 679.8 jit_solution(1722678336049449839)
XLA Ops:
  35.8 11.6 %all-to-all-done.2 = bf16[4,2,65536]{2,1,0:T(2,128)(2,1)S(1)} async-done(((bf16[4,2,65536]{2,1,0:T(2,128)(2,1)}), bf16[4,2,65536]{2,1,0:T(2,128)(2,1)S(1)}, u32[]{:S(2)}, u32[]{:S(2)}) %all-to-all-start.2) | async-done | bytes 1048608 | tf_op jit(solution)/shard_map/all_to_all | solution.py:84
  50.9 9.8 %copy.347 = bf16[2,32,4,2048]{3,2,1,0:T(4,128)(2,1)S(1)} copy(bf16[2,32,4,2048]{1,0,3,2:T(2,128)(2,1)} %bitcast.374) | data formatting | bytes 2097152 | tf_op jit(solution)/shard_map/all_to_all | solution.py:84
  68.7 16.4 %collective-permute-done.12 = bf16[128,2560]{1,0:T(8,128)(2,1)S(1)} collective-permute-done((bf16[128,2560]{1,0:T(8,128)(2,1)S(1)}, bf16[128,2560]{1,0:T(8,128)(2,1)S(1)}, u32[]{:S(2)}, u32[]{:S(2)}) %collective-permute-start.12) | collective-permute-done | bytes 655392 | tf_op jit(solution)/shard_map/ppermute | solution.py:19
  91.5 26.4 %collective-permute-done.13 = bf16[128,2560]{1,0:T(8,128)(2,1)S(1)} collective-permute-done((bf16[128,2560]{1,0:T(8,128)(2,1)S(1)}, bf16[128,2560]{1,0:T(8,128)(2,1)S(1)}, u32[]{:S(2)}, u32[]{:S(2)}) %collective-permute-start.13) | collective-permute-done | bytes 655392 | tf_op jit(solution)/shard_map/ppermute | solution.py:19
  134.9 29.1 %collective-permute-done.1 = bf16[128,512]{1,0:T(8,128)(2,1)S(1)} collective-permute-done((bf16[128,512]{1,0:T(8,128)(2,1)S(1)}, bf16[128,512]{1,0:T(8,128)(2,1)S(1)}, u32[]{:S(2)}, u32[]{:S(2)}) %collective-permute-start.1) | collective-permute-done | bytes 131104 | tf_op jit(solution)/shard_map/ppermute | solution.py:25
  164.1 14.2 %collective-permute-start.5 = (bf16[128,512]{1,0:T(8,128)(2,1)S(1)}, bf16[128,512]{1,0:T(8,128)(2,1)S(1)}, u32[]{:S(2)}, u32[]{:S(2)}) collective-permute-start(bf16[128,512]{1,0:T(8,128)(2,1)S(1)} %bitcast.389), channel_id=1, source_target_pairs={{0,24},{4,28},{8,32},{12,36},{16,40},{20,44},{24,48},{28,52},{32,5... | collective-permute-start | bytes 393224 | tf_op jit(solution)/shard_map/ppermute | solution.py:25
  186.0 10.9 %collective-permute-start.7 = (bf16[128,512]{1,0:T(8,128)(2,1)S(1)}, bf16[128,512]{1,0:T(8,128)(2,1)S(1)}, u32[]{:S(2)}, u32[]{:S(2)}) collective-permute-start(bf16[128,512]{1,0:T(8,128)(2,1)S(1)} %bitcast.391), channel_id=1, source_target_pairs={{0,16},{4,20},{8,24},{12,28},{16,32},{20,36},{24,40},{28,44},{32,4... | collective-permute-start | bytes 393224 | tf_op jit(solution)/shard_map/ppermute | solution.py:25
  197.0 23.4 %collective-permute-start.8 = (bf16[128,512]{1,0:T(8,128)(2,1)S(1)}, bf16[128,512]{1,0:T(8,128)(2,1)S(1)}, u32[]{:S(2)}, u32[]{:S(2)}) collective-permute-start(bf16[128,512]{1,0:T(8,128)(2,1)S(1)} %bitcast.392), channel_id=1, source_target_pairs={{0,12},{4,16},{8,20},{12,24},{16,28},{20,32},{24,36},{28,40},{32,4... | collective-permute-start | bytes 393224 | tf_op jit(solution)/shard_map/ppermute | solution.py:25
  233.4 26.2 %collective-permute-done.16 = bf16[128,2560]{1,0:T(8,128)(2,1)S(1)} collective-permute-done((bf16[128,2560]{1,0:T(8,128)(2,1)S(1)}, bf16[128,2560]{1,0:T(8,128)(2,1)S(1)}, u32[]{:S(2)}, u32[]{:S(2)}) %collective-permute-start.16) | collective-permute-done | bytes 655392 | tf_op jit(solution)/shard_map/ppermute | solution.py:19
  265.4 29.8 %collective-permute-done.17 = bf16[128,2560]{1,0:T(8,128)(2,1)S(1)} collective-permute-done((bf16[128,2560]{1,0:T(8,128)(2,1)S(1)}, bf16[128,2560]{1,0:T(8,128)(2,1)S(1)}, u32[]{:S(2)}, u32[]{:S(2)}) %collective-permute-start.17) | collective-permute-done | bytes 655392 | tf_op jit(solution)/shard_map/ppermute | solution.py:19
  318.0 14.0 %collective-permute-start.25 = (bf16[2,128,512]{2,1,0:T(8,128)(2,1)S(1)}, bf16[2,128,512]{2,1,0:T(8,128)(2,1)S(1)}, u32[]{:S(2)}, u32[]{:S(2)}) collective-permute-start(bf16[2,128,512]{2,1,0:T(8,128)(2,1)S(1)} %pad_maximum_fusion.3), channel_id=1, source_target_pairs={{32,0},{36,4},{40,8},{44,12},{48,16},{52,20},{56,24},{60,28},{64,3... | collective-permute-start | bytes 786440 | tf_op jit(solution)/shard_map/ppermute | solution.py:25
  332.7 71.5 %collective-permute-start.26 = (bf16[2,128,512]{2,1,0:T(8,128)(2,1)S(1)}, bf16[2,128,512]{2,1,0:T(8,128)(2,1)S(1)}, u32[]{:S(2)}, u32[]{:S(2)}) collective-permute-start(bf16[2,128,512]{2,1,0:T(8,128)(2,1)S(1)} %pad_maximum_fusion.3), channel_id=1, source_target_pairs={{36,0},{40,4},{44,8},{48,12},{52,16},{56,20},{60,24},{64,28},{68,3... | collective-permute-start | bytes 786440 | tf_op jit(solution)/shard_map/ppermute | solution.py:25
  420.2 15.3 %collective-permute-done.28 = bf16[2,128,512]{2,1,0:T(8,128)(2,1)S(1)} collective-permute-done((bf16[2,128,512]{2,1,0:T(8,128)(2,1)S(1)}, bf16[2,128,512]{2,1,0:T(8,128)(2,1)S(1)}, u32[]{:S(2)}, u32[]{:S(2)}) %collective-permute-start.28) | collective-permute-done | bytes 262176 | tf_op jit(solution)/shard_map/ppermute | solution.py:25
  462.4 9.1 %collective-permute-start.30 = (bf16[128,2048]{1,0:T(8,128)(2,1)S(1)}, bf16[128,2048]{1,0:T(8,128)(2,1)S(1)}, u32[]{:S(2)}, u32[]{:S(2)}) collective-permute-start(bf16[128,2048]{1,0:T(8,128)(2,1)S(1)} %collective-permute-done.29), channel_id=1, source_target_pairs={{0,8},{8,0},{4,12},{12,4},{16,24},{24,16},{20,28},{28,20},{32,40},... | collective-permute-start | bytes 1572872 | tf_op jit(solution)/shard_map/ppermute | solution.py:19
  471.5 12.2 %collective-permute-done.30 = bf16[128,2048]{1,0:T(8,128)(2,1)S(1)} collective-permute-done((bf16[128,2048]{1,0:T(8,128)(2,1)S(1)}, bf16[128,2048]{1,0:T(8,128)(2,1)S(1)}, u32[]{:S(2)}, u32[]{:S(2)}) %collective-permute-start.30) | collective-permute-done | bytes 524320 | tf_op jit(solution)/shard_map/ppermute | solution.py:19
  486.1 25.2 %collective-permute-done.31 = bf16[128,2048]{1,0:T(8,128)(2,1)} collective-permute-done((bf16[128,2048]{1,0:T(8,128)(2,1)S(1)}, bf16[128,2048]{1,0:T(8,128)(2,1)}, u32[]{:S(2)}, u32[]{:S(2)}) %collective-permute-start.31) | collective-permute-done | bytes 524320 | tf_op jit(solution)/shard_map/ppermute | solution.py:19
  517.5 21.3 %collective-permute-done.32 = bf16[128,2048]{1,0:T(8,128)(2,1)} collective-permute-done((bf16[128,2048]{1,0:T(8,128)(2,1)}, bf16[128,2048]{1,0:T(8,128)(2,1)}, u32[]{:S(2)}, u32[]{:S(2)}) %collective-permute-start.32) | collective-permute-done | bytes 524320 | tf_op jit(solution)/shard_map/ppermute | solution.py:19
  538.8 19.3 %collective-permute-start.33 = (bf16[128,2048]{1,0:T(8,128)(2,1)}, bf16[128,2048]{1,0:T(8,128)(2,1)}, u32[]{:S(2)}, u32[]{:S(2)}) collective-permute-start(bf16[128,2048]{1,0:T(8,128)(2,1)} %collective-permute-done.32), channel_id=1, source_target_pairs={{0,64},{64,0},{4,68},{68,4},{8,72},{72,8},{12,76},{76,12},{16,80},... | collective-permute-start | bytes 1572872 | tf_op jit(solution)/shard_map/ppermute | solution.py:19
  561.3 9.3 %collective-permute-done.33 = bf16[128,2048]{1,0:T(8,128)(2,1)} collective-permute-done((bf16[128,2048]{1,0:T(8,128)(2,1)}, bf16[128,2048]{1,0:T(8,128)(2,1)}, u32[]{:S(2)}, u32[]{:S(2)}) %collective-permute-start.33) | collective-permute-done | bytes 524320 | tf_op jit(solution)/shard_map/ppermute | solution.py:19
  570.5 9.3 %collective-permute-start.34 = (bf16[128,2048]{1,0:T(8,128)(2,1)}, bf16[128,2048]{1,0:T(8,128)(2,1)}, u32[]{:S(2)}, u32[]{:S(2)}) collective-permute-start(bf16[128,2048]{1,0:T(8,128)(2,1)} %collective-permute-done.33), channel_id=1, source_target_pairs={{0,128},{128,0},{4,132},{132,4},{8,136},{136,8},{12,140},{140,12},... | collective-permute-start | bytes 1572872 | tf_op jit(solution)/shard_map/ppermute | solution.py:19
  582.9 19.0 %collective-permute-done.34 = bf16[128,2048]{1,0:T(8,128)(2,1)} collective-permute-done((bf16[128,2048]{1,0:T(8,128)(2,1)}, bf16[128,2048]{1,0:T(8,128)(2,1)}, u32[]{:S(2)}, u32[]{:S(2)}) %collective-permute-start.34) | collective-permute-done | bytes 524320 | tf_op jit(solution)/shard_map/ppermute | solution.py:19
  601.9 34.6 %collective-permute-start.35 = (bf16[128,2048]{1,0:T(8,128)(2,1)}, bf16[128,2048]{1,0:T(8,128)(2,1)S(1)}, u32[]{:S(2)}, u32[]{:S(2)}) collective-permute-start(bf16[128,2048]{1,0:T(8,128)(2,1)} %collective-permute-done.34), channel_id=1, source_target_pairs={{0,256},{256,0},{4,260},{260,4},{8,264},{264,8},{12,268},{268,12},... | collective-permute-start | bytes 1572872 | tf_op jit(solution)/shard_map/ppermute | solution.py:19
  639.6 20.4 %collective-permute-done.35 = bf16[128,2048]{1,0:T(8,128)(2,1)S(1)} collective-permute-done((bf16[128,2048]{1,0:T(8,128)(2,1)}, bf16[128,2048]{1,0:T(8,128)(2,1)S(1)}, u32[]{:S(2)}, u32[]{:S(2)}) %collective-permute-start.35) | collective-permute-done | bytes 524320 | tf_op jit(solution)/shard_map/ppermute | solution.py:19
  661.1 17.3 %all_to_all.69 = bf16[2,128,2048]{2,0,1:T(2,128)(2,1)S(1)} all-to-all(bf16[2,128,2048]{2,0,1:T(2,128)(2,1)S(1)} %copy.317), channel_id=1, replica_groups=mesh['ctx'=128,'head'=4] {'head'}, dimensions={1} | all-to-all | bytes 2097152 | tf_op jit(solution)/shard_map/all_to_all | solution.py:130
  (185 shorter events, 183.1 us)
Async XLA Ops:
  85.1 32.8 %collective-permute-start.13 = (bf16[128,2560]{1,0:T(8,128)(2,1)S(1)}, bf16[128,2560]{1,0:T(8,128)(2,1)S(1)}, u32[]{:S(2)}, u32[]{:S(2)}) collective-permute-start(bf16[128,2560]{1,0:T(8,128)(2,1)S(1)} %collective-permute-done.12), channel_id=1, source_target_pairs={{0,16},{16,0},{4,20},{20,4},{8,24},{24,8},{12,28},{28,12},{32,48},... | collective-permute-start | bytes 1966088 | tf_op jit(solution)/shard_map/ppermute | solution.py:19
  90.2 41.7 %collective-permute-start = (bf16[128,512]{1,0:T(8,128)(2,1)S(1)}, bf16[128,512]{1,0:T(8,128)(2,1)S(1)}, u32[]{:S(2)}, u32[]{:S(2)}) collective-permute-start(bf16[128,512]{1,0:T(8,128)(2,1)S(1)} %bitcast.384), channel_id=1, source_target_pairs={{0,44},{4,48},{8,52},{12,56},{16,60},{20,64},{24,68},{28,72},{32,7... | collective-permute-start | bytes 393224 | tf_op jit(solution)/shard_map/ppermute | solution.py:25
  117.9 66.1 %collective-permute-start.14 = (bf16[128,2560]{1,0:T(8,128)(2,1)S(1)}, bf16[128,2560]{1,0:T(8,128)(2,1)S(1)}, u32[]{:S(2)}, u32[]{:S(2)}) collective-permute-start(bf16[128,2560]{1,0:T(8,128)(2,1)S(1)} %collective-permute-done.13), channel_id=1, source_target_pairs={{0,32},{32,0},{4,36},{36,4},{8,40},{40,8},{12,44},{44,12},{16,48},... | collective-permute-start | bytes 1966088 | tf_op jit(solution)/shard_map/ppermute | solution.py:19
  126.7 37.3 %collective-permute-start.1 = (bf16[128,512]{1,0:T(8,128)(2,1)S(1)}, bf16[128,512]{1,0:T(8,128)(2,1)S(1)}, u32[]{:S(2)}, u32[]{:S(2)}) collective-permute-start(bf16[128,512]{1,0:T(8,128)(2,1)S(1)} %bitcast.385), channel_id=1, source_target_pairs={{0,40},{4,44},{8,48},{12,52},{16,56},{20,60},{24,64},{28,68},{32,7... | collective-permute-start | bytes 393224 | tf_op jit(solution)/shard_map/ppermute | solution.py:25
  128.0 50.3 %collective-permute-start.2 = (bf16[128,512]{1,0:T(8,128)(2,1)S(1)}, bf16[128,512]{1,0:T(8,128)(2,1)S(1)}, u32[]{:S(2)}, u32[]{:S(2)}) collective-permute-start(bf16[128,512]{1,0:T(8,128)(2,1)S(1)} %bitcast.386), channel_id=1, source_target_pairs={{0,36},{4,40},{8,44},{12,48},{16,52},{20,56},{24,60},{28,64},{32,6... | collective-permute-start | bytes 393224 | tf_op jit(solution)/shard_map/ppermute | solution.py:25
  129.9 56.1 %collective-permute-start.3 = (bf16[128,512]{1,0:T(8,128)(2,1)S(1)}, bf16[128,512]{1,0:T(8,128)(2,1)S(1)}, u32[]{:S(2)}, u32[]{:S(2)}) collective-permute-start(bf16[128,512]{1,0:T(8,128)(2,1)S(1)} %bitcast.387), channel_id=1, source_target_pairs={{0,32},{4,36},{8,40},{12,44},{16,48},{20,52},{24,56},{28,60},{32,6... | collective-permute-start | bytes 393224 | tf_op jit(solution)/shard_map/ppermute | solution.py:25
  131.9 65.1 %collective-permute-start.4 = (bf16[128,512]{1,0:T(8,128)(2,1)S(1)}, bf16[128,512]{1,0:T(8,128)(2,1)S(1)}, u32[]{:S(2)}, u32[]{:S(2)}) collective-permute-start(bf16[128,512]{1,0:T(8,128)(2,1)S(1)} %bitcast.388), channel_id=1, source_target_pairs={{0,28},{4,32},{8,36},{12,40},{16,44},{20,48},{24,52},{28,56},{32,6... | collective-permute-start | bytes 393224 | tf_op jit(solution)/shard_map/ppermute | solution.py:25
  164.1 56.3 %collective-permute-start.5 = (bf16[128,512]{1,0:T(8,128)(2,1)S(1)}, bf16[128,512]{1,0:T(8,128)(2,1)S(1)}, u32[]{:S(2)}, u32[]{:S(2)}) collective-permute-start(bf16[128,512]{1,0:T(8,128)(2,1)S(1)} %bitcast.389), channel_id=1, source_target_pairs={{0,24},{4,28},{8,32},{12,36},{16,40},{20,44},{24,48},{28,52},{32,5... | collective-permute-start | bytes 393224 | tf_op jit(solution)/shard_map/ppermute | solution.py:25
  178.3 53.1 %collective-permute-start.6 = (bf16[128,512]{1,0:T(8,128)(2,1)S(1)}, bf16[128,512]{1,0:T(8,128)(2,1)S(1)}, u32[]{:S(2)}, u32[]{:S(2)}) collective-permute-start(bf16[128,512]{1,0:T(8,128)(2,1)S(1)} %bitcast.390), channel_id=1, source_target_pairs={{0,20},{4,24},{8,28},{12,32},{16,36},{20,40},{24,44},{28,48},{32,5... | collective-permute-start | bytes 393224 | tf_op jit(solution)/shard_map/ppermute | solution.py:25
  184.1 42.0 %collective-permute-start.15 = (bf16[128,2560]{1,0:T(8,128)(2,1)S(1)}, bf16[128,2560]{1,0:T(8,128)(2,1)S(1)}, u32[]{:S(2)}, u32[]{:S(2)}) collective-permute-start(bf16[128,2560]{1,0:T(8,128)(2,1)S(1)} %collective-permute-done.14), channel_id=1, source_target_pairs={{0,64},{64,0},{4,68},{68,4},{8,72},{72,8},{12,76},{76,12},{16,80},... | collective-permute-start | bytes 1966088 | tf_op jit(solution)/shard_map/ppermute | solution.py:19
  186.0 47.4 %collective-permute-start.7 = (bf16[128,512]{1,0:T(8,128)(2,1)S(1)}, bf16[128,512]{1,0:T(8,128)(2,1)S(1)}, u32[]{:S(2)}, u32[]{:S(2)}) collective-permute-start(bf16[128,512]{1,0:T(8,128)(2,1)S(1)} %bitcast.391), channel_id=1, source_target_pairs={{0,16},{4,20},{8,24},{12,28},{16,32},{20,36},{24,40},{28,44},{32,4... | collective-permute-start | bytes 393224 | tf_op jit(solution)/shard_map/ppermute | solution.py:25
  197.0 68.3 %collective-permute-start.8 = (bf16[128,512]{1,0:T(8,128)(2,1)S(1)}, bf16[128,512]{1,0:T(8,128)(2,1)S(1)}, u32[]{:S(2)}, u32[]{:S(2)}) collective-permute-start(bf16[128,512]{1,0:T(8,128)(2,1)S(1)} %bitcast.392), channel_id=1, source_target_pairs={{0,12},{4,16},{8,20},{12,24},{16,28},{20,32},{24,36},{28,40},{32,4... | collective-permute-start | bytes 393224 | tf_op jit(solution)/shard_map/ppermute | solution.py:25
  220.4 45.0 %collective-permute-start.9 = (bf16[128,512]{1,0:T(8,128)(2,1)S(1)}, bf16[128,512]{1,0:T(8,128)(2,1)S(1)}, u32[]{:S(2)}, u32[]{:S(2)}) collective-permute-start(bf16[128,512]{1,0:T(8,128)(2,1)S(1)} %bitcast.393), channel_id=1, source_target_pairs={{0,8},{4,12},{8,16},{12,20},{16,24},{20,28},{24,32},{28,36},{32,40... | collective-permute-start | bytes 393224 | tf_op jit(solution)/shard_map/ppermute | solution.py:25
  226.1 33.6 %collective-permute-start.16 = (bf16[128,2560]{1,0:T(8,128)(2,1)S(1)}, bf16[128,2560]{1,0:T(8,128)(2,1)S(1)}, u32[]{:S(2)}, u32[]{:S(2)}) collective-permute-start(bf16[128,2560]{1,0:T(8,128)(2,1)S(1)} %collective-permute-done.15), channel_id=1, source_target_pairs={{0,128},{128,0},{4,132},{132,4},{8,136},{136,8},{12,140},{140,12},... | collective-permute-start | bytes 1966088 | tf_op jit(solution)/shard_map/ppermute | solution.py:19
  231.4 33.9 %collective-permute-start.10 = (bf16[128,512]{1,0:T(8,128)(2,1)S(1)}, bf16[128,512]{1,0:T(8,128)(2,1)S(1)}, u32[]{:S(2)}, u32[]{:S(2)}) collective-permute-start(bf16[128,512]{1,0:T(8,128)(2,1)S(1)} %bitcast.394), channel_id=1, source_target_pairs={{0,4},{4,8},{8,12},{12,16},{16,20},{20,24},{24,28},{28,32},{32,36}... | collective-permute-start | bytes 393224 | tf_op jit(solution)/shard_map/ppermute | solution.py:25
  259.6 35.7 %collective-permute-start.17 = (bf16[128,2560]{1,0:T(8,128)(2,1)S(1)}, bf16[128,2560]{1,0:T(8,128)(2,1)S(1)}, u32[]{:S(2)}, u32[]{:S(2)}) collective-permute-start(bf16[128,2560]{1,0:T(8,128)(2,1)S(1)} %collective-permute-done.16), channel_id=1, source_target_pairs={{0,256},{256,0},{4,260},{260,4},{8,264},{264,8},{12,268},{268,12},... | collective-permute-start | bytes 1966088 | tf_op jit(solution)/shard_map/ppermute | solution.py:19
  306.7 98.1 %collective-permute-start.22 = (bf16[2,128,512]{2,1,0:T(8,128)(2,1)S(1)}, bf16[2,128,512]{2,1,0:T(8,128)(2,1)S(1)}, u32[]{:S(2)}, u32[]{:S(2)}) collective-permute-start(bf16[2,128,512]{2,1,0:T(8,128)(2,1)S(1)} %pad_maximum_fusion.3), channel_id=1, source_target_pairs={{20,0},{24,4},{28,8},{32,12},{36,16},{40,20},{44,24},{48,28},{52,3... | collective-permute-start | bytes 786440 | tf_op jit(solution)/shard_map/ppermute | solution.py:25
  311.1 97.7 %collective-permute-start.23 = (bf16[2,128,512]{2,1,0:T(8,128)(2,1)S(1)}, bf16[2,128,512]{2,1,0:T(8,128)(2,1)S(1)}, u32[]{:S(2)}, u32[]{:S(2)}) collective-permute-start(bf16[2,128,512]{2,1,0:T(8,128)(2,1)S(1)} %pad_maximum_fusion.3), channel_id=1, source_target_pairs={{24,0},{28,4},{32,8},{36,12},{40,16},{44,20},{48,24},{52,28},{56,3... | collective-permute-start | bytes 786440 | tf_op jit(solution)/shard_map/ppermute | solution.py:25
  314.9 99.4 %collective-permute-start.24 = (bf16[2,128,512]{2,1,0:T(8,128)(2,1)S(1)}, bf16[2,128,512]{2,1,0:T(8,128)(2,1)S(1)}, u32[]{:S(2)}, u32[]{:S(2)}) collective-permute-start(bf16[2,128,512]{2,1,0:T(8,128)(2,1)S(1)} %pad_maximum_fusion.3), channel_id=1, source_target_pairs={{28,0},{32,4},{36,8},{40,12},{44,16},{48,20},{52,24},{56,28},{60,3... | collective-permute-start | bytes 786440 | tf_op jit(solution)/shard_map/ppermute | solution.py:25
  318.0 96.9 %collective-permute-start.25 = (bf16[2,128,512]{2,1,0:T(8,128)(2,1)S(1)}, bf16[2,128,512]{2,1,0:T(8,128)(2,1)S(1)}, u32[]{:S(2)}, u32[]{:S(2)}) collective-permute-start(bf16[2,128,512]{2,1,0:T(8,128)(2,1)S(1)} %pad_maximum_fusion.3), channel_id=1, source_target_pairs={{32,0},{36,4},{40,8},{44,12},{48,16},{52,20},{56,24},{60,28},{64,3... | collective-permute-start | bytes 786440 | tf_op jit(solution)/shard_map/ppermute | solution.py:25
  332.7 82.9 %collective-permute-start.26 = (bf16[2,128,512]{2,1,0:T(8,128)(2,1)S(1)}, bf16[2,128,512]{2,1,0:T(8,128)(2,1)S(1)}, u32[]{:S(2)}, u32[]{:S(2)}) collective-permute-start(bf16[2,128,512]{2,1,0:T(8,128)(2,1)S(1)} %pad_maximum_fusion.3), channel_id=1, source_target_pairs={{36,0},{40,4},{44,8},{48,12},{52,16},{56,20},{60,24},{64,28},{68,3... | collective-permute-start | bytes 786440 | tf_op jit(solution)/shard_map/ppermute | solution.py:25
  538.8 31.7 %collective-permute-start.33 = (bf16[128,2048]{1,0:T(8,128)(2,1)}, bf16[128,2048]{1,0:T(8,128)(2,1)}, u32[]{:S(2)}, u32[]{:S(2)}) collective-permute-start(bf16[128,2048]{1,0:T(8,128)(2,1)} %collective-permute-done.32), channel_id=1, source_target_pairs={{0,64},{64,0},{4,68},{68,4},{8,72},{72,8},{12,76},{76,12},{16,80},... | collective-permute-start | bytes 1572872 | tf_op jit(solution)/shard_map/ppermute | solution.py:19
  570.5 31.4 %collective-permute-start.34 = (bf16[128,2048]{1,0:T(8,128)(2,1)}, bf16[128,2048]{1,0:T(8,128)(2,1)}, u32[]{:S(2)}, u32[]{:S(2)}) collective-permute-start(bf16[128,2048]{1,0:T(8,128)(2,1)} %collective-permute-done.33), channel_id=1, source_target_pairs={{0,128},{128,0},{4,132},{132,4},{8,136},{136,8},{12,140},{140,12},... | collective-permute-start | bytes 1572872 | tf_op jit(solution)/shard_map/ppermute | solution.py:19
  601.9 58.0 %collective-permute-start.35 = (bf16[128,2048]{1,0:T(8,128)(2,1)}, bf16[128,2048]{1,0:T(8,128)(2,1)S(1)}, u32[]{:S(2)}, u32[]{:S(2)}) collective-permute-start(bf16[128,2048]{1,0:T(8,128)(2,1)} %collective-permute-done.34), channel_id=1, source_target_pairs={{0,256},{256,0},{4,260},{260,4},{8,264},{264,8},{12,268},{268,12},... | collective-permute-start | bytes 1572872 | tf_op jit(solution)/shard_map/ppermute | solution.py:19
  (27 other events, 417.1 us)
where the time goes:
time: 682 us; the launch traced here: 680 us
  starting transfers between devices  303 us (44%)
  waiting for transfers between devices  273 us (40%)
  local copies, waits for them, and re-layouts  53.2 us (8%)
  matrix products  25.2 us (4%)
  blocking collectives  17.3 us (3%)
  other arithmetic  7.01 us (1%)
    ppermute x14, waiting for transfers between devices, partner(): return lax.ppermute(block, axis, route)  210 us
    ppermute x22, starting transfers between devices, shifted(): return lax.ppermute(block, axis, route)  182 us
    ppermute x14, starting transfers between devices, partner(): return lax.ppermute(block, axis, route)  109 us
    ppermute x22, waiting for transfers between devices, shifted(): return lax.ppermute(block, axis, route)  47.8 us
    unnamed x55, local copies, waits for them, and re-layouts  30 us
    all_to_all x1, blocking collectives, per_device(): lax.all_to_all(result, 'head', split_axis=1, concat_axis=2, tiled=True)  17.3 us
  transfers between devices with their start and end apart: 39, of which 17 were waited for; matrix products, arithmetic and copies ran while one was open for 7% of the time, Pallas kernels for 0%

commit v1 on v0

--- a/solution.py
+++ b/solution.py
@@ -81,7 +81,12 @@
     ctx_pos = lax.axis_index("ctx")
     reach = min(REACH, ctx_count // 2)
     query_local, key_local, value_local = (
-        lax.all_to_all(queries, "head", split_axis=2, concat_axis=1, tiled=True),
+        jnp.concatenate(
+            lax.all_to_all(
+                jnp.stack(jnp.split(queries, lax.axis_size("head"), axis=2)), "head", 0, 0
+            ),
+            axis=1,
+        ),
         lax.all_to_all(keys, "head", split_axis=2, concat_axis=1, tiled=True),
         lax.all_to_all(values, "head", split_axis=2, concat_axis=1, tiled=True),
     )

time: 682 us -> 658 us (0.965)
  local copies, waits for them, and re-layouts: 53.2 us -> 33.8 us
  waiting for transfers between devices: 273 us -> 261 us
  matrix products: 25.2 us -> 32.5 us
    ppermute x14, waiting for transfers between devices: 210 us -> 196 us  [partner(): return lax.ppermute(block, axis, route)]
    unnamed x55 -> x48, local copies, waits for them, and re-layouts: 30 us -> 19.4 us
    all_to_all x1, local copies, waits for them, and re-layouts: 9.82 us -> 0.1 us  [per_device(): lax.all_to_all(jnp.stack(jnp.split(queries, lax.axis_size('head'), axis=2...]
  transfers between devices with their start and end apart: 39 -> 39, of which waited for: 17 -> 18; matrix products, arithmetic and copies ran while one was open for 7% -> 7% of each run, Pallas kernels for 0% -> 0%
where the time goes in v1:
time: 658 us; the launch traced here: 656 us
  starting transfers between devices  303 us (46%)
  waiting for transfers between devices  261 us (40%)
  local copies, waits for them, and re-layouts  33.8 us (5%)
  matrix products  32.5 us (5%)
  blocking collectives  17.3 us (3%)
  other arithmetic  8.11 us (1%)
    ppermute x14, waiting for transfers between devices, partner(): return lax.ppermute(block, axis, route)  196 us
    ppermute x22, starting transfers between devices, shifted(): return lax.ppermute(block, axis, route)  179 us
    ppermute x14, starting transfers between devices, partner(): return lax.ppermute(block, axis, route)  113 us
    ppermute x22, waiting for transfers between devices, shifted(): return lax.ppermute(block, axis, route)  45.4 us
    unnamed x48, local copies, waits for them, and re-layouts  19.4 us
    all_to_all x1, blocking collectives, per_device(): lax.all_to_all(result, 'head', split_axis=1, concat_axis=2, tiled=True)  17.3 us
    sub x8, matrix products, attend(): weights = jnp.where(allowed[None], jnp.exp(masked - top), 0.0)  16.4 us
    dot_general x8, matrix products, attend(): jnp.einsum('hrs,sd->rhd', weights.astype(jnp.bfloat16), value_head, prefe...  16.1 us
  transfers between devices with their start and end apart: 39, of which 18 were waited for; matrix products, arithmetic and copies ran while one was open for 7% of the time, Pallas kernels for 0%

profile of v1, /device:TPU:248, one launch (start us, length us, event | category | flops | bytes accessed | tf_op | source)
XLA Modules:
  0.0 656.0 jit_solution(9942297207105084641)
XLA Ops:
  27.3 11.0 %all-to-all-done.2 = bf16[4,2,32,2048]{3,2,1,0:T(8,128)(2,1)S(1)} async-done(((bf16[4,2,32,2048]{3,2,1,0:T(8,128)(2,1)}), bf16[4,2,32,2048]{3,2,1,0:T(8,128)(2,1)S(1)}, u32[]{:S(2)}, u32[]{:S(2)}) %all-to-all-start.2) | async-done | bytes 1048608 | tf_op jit(solution)/shard_map/all_to_all | solution.py:85
  45.5 16.4 %collective-permute-done.12 = bf16[128,2560]{1,0:T(8,128)(2,1)S(1)} collective-permute-done((bf16[128,2560]{1,0:T(8,128)(2,1)S(1)}, bf16[128,2560]{1,0:T(8,128)(2,1)S(1)}, u32[]{:S(2)}, u32[]{:S(2)}) %collective-permute-start.12) | collective-permute-done | bytes 655392 | tf_op jit(solution)/shard_map/ppermute | solution.py:19
  68.3 26.4 %collective-permute-done.13 = bf16[128,2560]{1,0:T(8,128)(2,1)S(1)} collective-permute-done((bf16[128,2560]{1,0:T(8,128)(2,1)S(1)}, bf16[128,2560]{1,0:T(8,128)(2,1)S(1)}, u32[]{:S(2)}, u32[]{:S(2)}) %collective-permute-start.13) | collective-permute-done | bytes 655392 | tf_op jit(solution)/shard_map/ppermute | solution.py:19
  94.7 8.2 %collective-permute-start.14 = (bf16[128,2560]{1,0:T(8,128)(2,1)S(1)}, bf16[128,2560]{1,0:T(8,128)(2,1)S(1)}, u32[]{:S(2)}, u32[]{:S(2)}) collective-permute-start(bf16[128,2560]{1,0:T(8,128)(2,1)S(1)} %collective-permute-done.13), channel_id=1, source_target_pairs={{0,32},{32,0},{4,36},{36,4},{8,40},{40,8},{12,44},{44,12},{16,48},... | collective-permute-start | bytes 1966088 | tf_op jit(solution)/shard_map/ppermute | solution.py:19
  112.4 28.5 %collective-permute-done.1 = bf16[128,512]{1,0:T(8,128)(2,1)S(1)} collective-permute-done((bf16[128,512]{1,0:T(8,128)(2,1)S(1)}, bf16[128,512]{1,0:T(8,128)(2,1)S(1)}, u32[]{:S(2)}, u32[]{:S(2)}) %collective-permute-start.1) | collective-permute-done | bytes 131104 | tf_op jit(solution)/shard_map/ppermute | solution.py:25
  140.8 14.2 %collective-permute-start.5 = (bf16[128,512]{1,0:T(8,128)(2,1)S(1)}, bf16[128,512]{1,0:T(8,128)(2,1)S(1)}, u32[]{:S(2)}, u32[]{:S(2)}) collective-permute-start(bf16[128,512]{1,0:T(8,128)(2,1)S(1)} %bitcast.394), channel_id=1, source_target_pairs={{0,24},{4,28},{8,32},{12,36},{16,40},{20,44},{24,48},{28,52},{32,5... | collective-permute-start | bytes 393224 | tf_op jit(solution)/shard_map/ppermute | solution.py:25
  163.5 10.9 %collective-permute-start.7 = (bf16[128,512]{1,0:T(8,128)(2,1)S(1)}, bf16[128,512]{1,0:T(8,128)(2,1)S(1)}, u32[]{:S(2)}, u32[]{:S(2)}) collective-permute-start(bf16[128,512]{1,0:T(8,128)(2,1)S(1)} %bitcast.396), channel_id=1, source_target_pairs={{0,16},{4,20},{8,24},{12,28},{16,32},{20,36},{24,40},{28,44},{32,4... | collective-permute-start | bytes 393224 | tf_op jit(solution)/shard_map/ppermute | solution.py:25
  175.0 23.3 %collective-permute-start.8 = (bf16[128,512]{1,0:T(8,128)(2,1)S(1)}, bf16[128,512]{1,0:T(8,128)(2,1)S(1)}, u32[]{:S(2)}, u32[]{:S(2)}) collective-permute-start(bf16[128,512]{1,0:T(8,128)(2,1)S(1)} %bitcast.397), channel_id=1, source_target_pairs={{0,12},{4,16},{8,20},{12,24},{16,28},{20,32},{24,36},{28,40},{32,4... | collective-permute-start | bytes 393224 | tf_op jit(solution)/shard_map/ppermute | solution.py:25
  214.0 24.3 %collective-permute-done.16 = bf16[128,2560]{1,0:T(8,128)(2,1)S(1)} collective-permute-done((bf16[128,2560]{1,0:T(8,128)(2,1)S(1)}, bf16[128,2560]{1,0:T(8,128)(2,1)S(1)}, u32[]{:S(2)}, u32[]{:S(2)}) %collective-permute-start.16) | collective-permute-done | bytes 655392 | tf_op jit(solution)/shard_map/ppermute | solution.py:19
  246.1 28.0 %collective-permute-done.17 = bf16[128,2560]{1,0:T(8,128)(2,1)S(1)} collective-permute-done((bf16[128,2560]{1,0:T(8,128)(2,1)S(1)}, bf16[128,2560]{1,0:T(8,128)(2,1)S(1)}, u32[]{:S(2)}, u32[]{:S(2)}) %collective-permute-start.17) | collective-permute-done | bytes 655392 | tf_op jit(solution)/shard_map/ppermute | solution.py:19
  311.6 43.4 %collective-permute-start.26 = (bf16[2,128,512]{2,1,0:T(8,128)(2,1)S(1)}, bf16[2,128,512]{2,1,0:T(8,128)(2,1)S(1)}, u32[]{:S(2)}, u32[]{:S(2)}) collective-permute-start(bf16[2,128,512]{2,1,0:T(8,128)(2,1)S(1)} %pad_maximum_fusion.4), channel_id=1, source_target_pairs={{36,0},{40,4},{44,8},{48,12},{52,16},{56,20},{60,24},{64,28},{68,3... | collective-permute-start | bytes 786440 | tf_op jit(solution)/shard_map/ppermute | solution.py:25
  360.5 35.7 %collective-permute-start.28 = (bf16[2,128,512]{2,1,0:T(8,128)(2,1)S(1)}, bf16[2,128,512]{2,1,0:T(8,128)(2,1)S(1)}, u32[]{:S(2)}, u32[]{:S(2)}) collective-permute-start(bf16[2,128,512]{2,1,0:T(8,128)(2,1)S(1)} %pad_maximum_fusion.4), channel_id=1, source_target_pairs={{44,0},{48,4},{52,8},{56,12},{60,16},{64,20},{68,24},{72,28},{76,3... | collective-permute-start | bytes 786440 | tf_op jit(solution)/shard_map/ppermute | solution.py:25
  399.6 10.8 %collective-permute-done.28 = bf16[2,128,512]{2,1,0:T(8,128)(2,1)S(1)} collective-permute-done((bf16[2,128,512]{2,1,0:T(8,128)(2,1)S(1)}, bf16[2,128,512]{2,1,0:T(8,128)(2,1)S(1)}, u32[]{:S(2)}, u32[]{:S(2)}) %collective-permute-start.28) | collective-permute-done | bytes 262176 | tf_op jit(solution)/shard_map/ppermute | solution.py:25
  434.2 6.9 %collective-permute-start.30 = (bf16[128,2048]{1,0:T(8,128)(2,1)S(1)}, bf16[128,2048]{1,0:T(8,128)(2,1)S(1)}, u32[]{:S(2)}, u32[]{:S(2)}) collective-permute-start(bf16[128,2048]{1,0:T(8,128)(2,1)S(1)} %collective-permute-done.29), channel_id=1, source_target_pairs={{0,8},{8,0},{4,12},{12,4},{16,24},{24,16},{20,28},{28,20},{32,40},... | collective-permute-start | bytes 1572872 | tf_op jit(solution)/shard_map/ppermute | solution.py:19
  441.1 12.2 %collective-permute-done.30 = bf16[128,2048]{1,0:T(8,128)(2,1)S(1)} collective-permute-done((bf16[128,2048]{1,0:T(8,128)(2,1)S(1)}, bf16[128,2048]{1,0:T(8,128)(2,1)S(1)}, u32[]{:S(2)}, u32[]{:S(2)}) %collective-permute-start.30) | collective-permute-done | bytes 524320 | tf_op jit(solution)/shard_map/ppermute | solution.py:19
  459.1 22.7 %collective-permute-done.31 = bf16[128,2048]{1,0:T(8,128)(2,1)S(1)} collective-permute-done((bf16[128,2048]{1,0:T(8,128)(2,1)S(1)}, bf16[128,2048]{1,0:T(8,128)(2,1)S(1)}, u32[]{:S(2)}, u32[]{:S(2)}) %collective-permute-start.31) | collective-permute-done | bytes 524320 | tf_op jit(solution)/shard_map/ppermute | solution.py:19
  488.9 21.0 %collective-permute-done.32 = bf16[128,2048]{1,0:T(8,128)(2,1)S(1)} collective-permute-done((bf16[128,2048]{1,0:T(8,128)(2,1)S(1)}, bf16[128,2048]{1,0:T(8,128)(2,1)S(1)}, u32[]{:S(2)}, u32[]{:S(2)}) %collective-permute-start.32) | collective-permute-done | bytes 524320 | tf_op jit(solution)/shard_map/ppermute | solution.py:19
  509.9 21.6 %collective-permute-start.33 = (bf16[128,2048]{1,0:T(8,128)(2,1)S(1)}, bf16[128,2048]{1,0:T(8,128)(2,1)S(1)}, u32[]{:S(2)}, u32[]{:S(2)}) collective-permute-start(bf16[128,2048]{1,0:T(8,128)(2,1)S(1)} %collective-permute-done.32), channel_id=1, source_target_pairs={{0,64},{64,0},{4,68},{68,4},{8,72},{72,8},{12,76},{76,12},{16,80},... | collective-permute-start | bytes 1572872 | tf_op jit(solution)/shard_map/ppermute | solution.py:19
  536.7 6.9 %collective-permute-done.33 = bf16[128,2048]{1,0:T(8,128)(2,1)S(1)} collective-permute-done((bf16[128,2048]{1,0:T(8,128)(2,1)S(1)}, bf16[128,2048]{1,0:T(8,128)(2,1)S(1)}, u32[]{:S(2)}, u32[]{:S(2)}) %collective-permute-start.33) | collective-permute-done | bytes 524320 | tf_op jit(solution)/shard_map/ppermute | solution.py:19
  543.6 14.3 %collective-permute-start.34 = (bf16[128,2048]{1,0:T(8,128)(2,1)S(1)}, bf16[128,2048]{1,0:T(8,128)(2,1)S(1)}, u32[]{:S(2)}, u32[]{:S(2)}) collective-permute-start(bf16[128,2048]{1,0:T(8,128)(2,1)S(1)} %collective-permute-done.33), channel_id=1, source_target_pairs={{0,128},{128,0},{4,132},{132,4},{8,136},{136,8},{12,140},{140,12},... | collective-permute-start | bytes 1572872 | tf_op jit(solution)/shard_map/ppermute | solution.py:19
  563.1 16.6 %collective-permute-done.34 = bf16[128,2048]{1,0:T(8,128)(2,1)S(1)} collective-permute-done((bf16[128,2048]{1,0:T(8,128)(2,1)S(1)}, bf16[128,2048]{1,0:T(8,128)(2,1)S(1)}, u32[]{:S(2)}, u32[]{:S(2)}) %collective-permute-start.34) | collective-permute-done | bytes 524320 | tf_op jit(solution)/shard_map/ppermute | solution.py:19
  579.7 33.3 %collective-permute-start.35 = (bf16[128,2048]{1,0:T(8,128)(2,1)S(1)}, bf16[128,2048]{1,0:T(8,128)(2,1)S(1)}, u32[]{:S(2)}, u32[]{:S(2)}) collective-permute-start(bf16[128,2048]{1,0:T(8,128)(2,1)S(1)} %collective-permute-done.34), channel_id=1, source_target_pairs={{0,256},{256,0},{4,260},{260,4},{8,264},{264,8},{12,268},{268,12},... | collective-permute-start | bytes 1572872 | tf_op jit(solution)/shard_map/ppermute | solution.py:19
  618.1 18.0 %collective-permute-done.35 = bf16[128,2048]{1,0:T(8,128)(2,1)S(1)} collective-permute-done((bf16[128,2048]{1,0:T(8,128)(2,1)S(1)}, bf16[128,2048]{1,0:T(8,128)(2,1)S(1)}, u32[]{:S(2)}, u32[]{:S(2)}) %collective-permute-start.35) | collective-permute-done | bytes 524320 | tf_op jit(solution)/shard_map/ppermute | solution.py:19
  637.3 17.3 %all_to_all.59 = bf16[2,128,2048]{2,0,1:T(2,128)(2,1)S(1)} all-to-all(bf16[2,128,2048]{2,0,1:T(2,128)(2,1)S(1)} %copy.300), channel_id=1, replica_groups=mesh['ctx'=128,'head'=4] {'head'}, dimensions={1} | all-to-all | bytes 2097152 | tf_op jit(solution)/shard_map/all_to_all | solution.py:135
  (178 shorter events, 183.3 us)
Async XLA Ops:
  67.0 41.7 %collective-permute-start = (bf16[128,512]{1,0:T(8,128)(2,1)S(1)}, bf16[128,512]{1,0:T(8,128)(2,1)S(1)}, u32[]{:S(2)}, u32[]{:S(2)}) collective-permute-start(bf16[128,512]{1,0:T(8,128)(2,1)S(1)} %bitcast.389), channel_id=1, source_target_pairs={{0,44},{4,48},{8,52},{12,56},{16,60},{20,64},{24,68},{28,72},{32,7... | collective-permute-start | bytes 393224 | tf_op jit(solution)/shard_map/ppermute | solution.py:25
  94.7 66.1 %collective-permute-start.14 = (bf16[128,2560]{1,0:T(8,128)(2,1)S(1)}, bf16[128,2560]{1,0:T(8,128)(2,1)S(1)}, u32[]{:S(2)}, u32[]{:S(2)}) collective-permute-start(bf16[128,2560]{1,0:T(8,128)(2,1)S(1)} %collective-permute-done.13), channel_id=1, source_target_pairs={{0,32},{32,0},{4,36},{36,4},{8,40},{40,8},{12,44},{44,12},{16,48},... | collective-permute-start | bytes 1966088 | tf_op jit(solution)/shard_map/ppermute | solution.py:19
  103.5 37.3 %collective-permute-start.1 = (bf16[128,512]{1,0:T(8,128)(2,1)S(1)}, bf16[128,512]{1,0:T(8,128)(2,1)S(1)}, u32[]{:S(2)}, u32[]{:S(2)}) collective-permute-start(bf16[128,512]{1,0:T(8,128)(2,1)S(1)} %bitcast.390), channel_id=1, source_target_pairs={{0,40},{4,44},{8,48},{12,52},{16,56},{20,60},{24,64},{28,68},{32,7... | collective-permute-start | bytes 393224 | tf_op jit(solution)/shard_map/ppermute | solution.py:25
  104.8 50.9 %collective-permute-start.2 = (bf16[128,512]{1,0:T(8,128)(2,1)S(1)}, bf16[128,512]{1,0:T(8,128)(2,1)S(1)}, u32[]{:S(2)}, u32[]{:S(2)}) collective-permute-start(bf16[128,512]{1,0:T(8,128)(2,1)S(1)} %bitcast.391), channel_id=1, source_target_pairs={{0,36},{4,40},{8,44},{12,48},{16,52},{20,56},{24,60},{28,64},{32,6... | collective-permute-start | bytes 393224 | tf_op jit(solution)/shard_map/ppermute | solution.py:25
  106.7 56.7 %collective-permute-start.3 = (bf16[128,512]{1,0:T(8,128)(2,1)S(1)}, bf16[128,512]{1,0:T(8,128)(2,1)S(1)}, u32[]{:S(2)}, u32[]{:S(2)}) collective-permute-start(bf16[128,512]{1,0:T(8,128)(2,1)S(1)} %bitcast.392), channel_id=1, source_target_pairs={{0,32},{4,36},{8,40},{12,44},{16,48},{20,52},{24,56},{28,60},{32,6... | collective-permute-start | bytes 393224 | tf_op jit(solution)/shard_map/ppermute | solution.py:25
  108.7 66.3 %collective-permute-start.4 = (bf16[128,512]{1,0:T(8,128)(2,1)S(1)}, bf16[128,512]{1,0:T(8,128)(2,1)S(1)}, u32[]{:S(2)}, u32[]{:S(2)}) collective-permute-start(bf16[128,512]{1,0:T(8,128)(2,1)S(1)} %bitcast.393), channel_id=1, source_target_pairs={{0,28},{4,32},{8,36},{12,40},{16,44},{20,48},{24,52},{28,56},{32,6... | collective-permute-start | bytes 393224 | tf_op jit(solution)/shard_map/ppermute | solution.py:25
  140.8 58.2 %collective-permute-start.5 = (bf16[128,512]{1,0:T(8,128)(2,1)S(1)}, bf16[128,512]{1,0:T(8,128)(2,1)S(1)}, u32[]{:S(2)}, u32[]{:S(2)}) collective-permute-start(bf16[128,512]{1,0:T(8,128)(2,1)S(1)} %bitcast.394), channel_id=1, source_target_pairs={{0,24},{4,28},{8,32},{12,36},{16,40},{20,44},{24,48},{28,52},{32,5... | collective-permute-start | bytes 393224 | tf_op jit(solution)/shard_map/ppermute | solution.py:25
  155.8 55.0 %collective-permute-start.6 = (bf16[128,512]{1,0:T(8,128)(2,1)S(1)}, bf16[128,512]{1,0:T(8,128)(2,1)S(1)}, u32[]{:S(2)}, u32[]{:S(2)}) collective-permute-start(bf16[128,512]{1,0:T(8,128)(2,1)S(1)} %bitcast.395), channel_id=1, source_target_pairs={{0,20},{4,24},{8,28},{12,32},{16,36},{20,40},{24,44},{28,48},{32,5... | collective-permute-start | bytes 393224 | tf_op jit(solution)/shard_map/ppermute | solution.py:25
  160.9 43.8 %collective-permute-start.15 = (bf16[128,2560]{1,0:T(8,128)(2,1)S(1)}, bf16[128,2560]{1,0:T(8,128)(2,1)S(1)}, u32[]{:S(2)}, u32[]{:S(2)}) collective-permute-start(bf16[128,2560]{1,0:T(8,128)(2,1)S(1)} %collective-permute-done.14), channel_id=1, source_target_pairs={{0,64},{64,0},{4,68},{68,4},{8,72},{72,8},{12,76},{76,12},{16,80},... | collective-permute-start | bytes 1966088 | tf_op jit(solution)/shard_map/ppermute | solution.py:19
  163.5 49.9 %collective-permute-start.7 = (bf16[128,512]{1,0:T(8,128)(2,1)S(1)}, bf16[128,512]{1,0:T(8,128)(2,1)S(1)}, u32[]{:S(2)}, u32[]{:S(2)}) collective-permute-start(bf16[128,512]{1,0:T(8,128)(2,1)S(1)} %bitcast.396), channel_id=1, source_target_pairs={{0,16},{4,20},{8,24},{12,28},{16,32},{20,36},{24,40},{28,44},{32,4... | collective-permute-start | bytes 393224 | tf_op jit(solution)/shard_map/ppermute | solution.py:25
  175.0 69.1 %collective-permute-start.8 = (bf16[128,512]{1,0:T(8,128)(2,1)S(1)}, bf16[128,512]{1,0:T(8,128)(2,1)S(1)}, u32[]{:S(2)}, u32[]{:S(2)}) collective-permute-start(bf16[128,512]{1,0:T(8,128)(2,1)S(1)} %bitcast.397), channel_id=1, source_target_pairs={{0,12},{4,16},{8,20},{12,24},{16,28},{20,32},{24,36},{28,40},{32,4... | collective-permute-start | bytes 393224 | tf_op jit(solution)/shard_map/ppermute | solution.py:25
  199.0 45.8 %collective-permute-start.9 = (bf16[128,512]{1,0:T(8,128)(2,1)S(1)}, bf16[128,512]{1,0:T(8,128)(2,1)S(1)}, u32[]{:S(2)}, u32[]{:S(2)}) collective-permute-start(bf16[128,512]{1,0:T(8,128)(2,1)S(1)} %bitcast.398), channel_id=1, source_target_pairs={{0,8},{4,12},{8,16},{12,20},{16,24},{20,28},{24,32},{28,36},{32,40... | collective-permute-start | bytes 393224 | tf_op jit(solution)/shard_map/ppermute | solution.py:25
  210.8 34.7 %collective-permute-start.10 = (bf16[128,512]{1,0:T(8,128)(2,1)S(1)}, bf16[128,512]{1,0:T(8,128)(2,1)S(1)}, u32[]{:S(2)}, u32[]{:S(2)}) collective-permute-start(bf16[128,512]{1,0:T(8,128)(2,1)S(1)} %bitcast.399), channel_id=1, source_target_pairs={{0,4},{4,8},{8,12},{12,16},{16,20},{20,24},{24,28},{28,32},{32,36}... | collective-permute-start | bytes 393224 | tf_op jit(solution)/shard_map/ppermute | solution.py:25
  238.3 35.7 %collective-permute-start.17 = (bf16[128,2560]{1,0:T(8,128)(2,1)S(1)}, bf16[128,2560]{1,0:T(8,128)(2,1)S(1)}, u32[]{:S(2)}, u32[]{:S(2)}) collective-permute-start(bf16[128,2560]{1,0:T(8,128)(2,1)S(1)} %collective-permute-done.16), channel_id=1, source_target_pairs={{0,256},{256,0},{4,260},{260,4},{8,264},{264,8},{12,268},{268,12},... | collective-permute-start | bytes 1966088 | tf_op jit(solution)/shard_map/ppermute | solution.py:19
  286.1 69.6 %collective-permute-start.22 = (bf16[2,128,512]{2,1,0:T(8,128)(2,1)S(1)}, bf16[2,128,512]{2,1,0:T(8,128)(2,1)S(1)}, u32[]{:S(2)}, u32[]{:S(2)}) collective-permute-start(bf16[2,128,512]{2,1,0:T(8,128)(2,1)S(1)} %pad_maximum_fusion.4), channel_id=1, source_target_pairs={{20,0},{24,4},{28,8},{32,12},{36,16},{40,20},{44,24},{48,28},{52,3... | collective-permute-start | bytes 786440 | tf_op jit(solution)/shard_map/ppermute | solution.py:25
  290.5 70.0 %collective-permute-start.23 = (bf16[2,128,512]{2,1,0:T(8,128)(2,1)S(1)}, bf16[2,128,512]{2,1,0:T(8,128)(2,1)S(1)}, u32[]{:S(2)}, u32[]{:S(2)}) collective-permute-start(bf16[2,128,512]{2,1,0:T(8,128)(2,1)S(1)} %pad_maximum_fusion.4), channel_id=1, source_target_pairs={{24,0},{28,4},{32,8},{36,12},{40,16},{44,20},{48,24},{52,28},{56,3... | collective-permute-start | bytes 786440 | tf_op jit(solution)/shard_map/ppermute | solution.py:25
  294.3 102.6 %collective-permute-start.24 = (bf16[2,128,512]{2,1,0:T(8,128)(2,1)S(1)}, bf16[2,128,512]{2,1,0:T(8,128)(2,1)S(1)}, u32[]{:S(2)}, u32[]{:S(2)}) collective-permute-start(bf16[2,128,512]{2,1,0:T(8,128)(2,1)S(1)} %pad_maximum_fusion.4), channel_id=1, source_target_pairs={{28,0},{32,4},{36,8},{40,12},{44,16},{48,20},{52,24},{56,28},{60,3... | collective-permute-start | bytes 786440 | tf_op jit(solution)/shard_map/ppermute | solution.py:25
  304.3 93.3 %collective-permute-start.25 = (bf16[2,128,512]{2,1,0:T(8,128)(2,1)S(1)}, bf16[2,128,512]{2,1,0:T(8,128)(2,1)S(1)}, u32[]{:S(2)}, u32[]{:S(2)}) collective-permute-start(bf16[2,128,512]{2,1,0:T(8,128)(2,1)S(1)} %pad_maximum_fusion.4), channel_id=1, source_target_pairs={{32,0},{36,4},{40,8},{44,12},{48,16},{52,20},{56,24},{60,28},{64,3... | collective-permute-start | bytes 786440 | tf_op jit(solution)/shard_map/ppermute | solution.py:25
  311.6 86.6 %collective-permute-start.26 = (bf16[2,128,512]{2,1,0:T(8,128)(2,1)S(1)}, bf16[2,128,512]{2,1,0:T(8,128)(2,1)S(1)}, u32[]{:S(2)}, u32[]{:S(2)}) collective-permute-start(bf16[2,128,512]{2,1,0:T(8,128)(2,1)S(1)} %pad_maximum_fusion.4), channel_id=1, source_target_pairs={{36,0},{40,4},{44,8},{48,12},{52,16},{56,20},{60,24},{64,28},{68,3... | collective-permute-start | bytes 786440 | tf_op jit(solution)/shard_map/ppermute | solution.py:25
  355.7 43.2 %collective-permute-start.27 = (bf16[2,128,512]{2,1,0:T(8,128)(2,1)S(1)}, bf16[2,128,512]{2,1,0:T(8,128)(2,1)S(1)}, u32[]{:S(2)}, u32[]{:S(2)}) collective-permute-start(bf16[2,128,512]{2,1,0:T(8,128)(2,1)S(1)} %pad_maximum_fusion.4), channel_id=1, source_target_pairs={{40,0},{44,4},{48,8},{52,12},{56,16},{60,20},{64,24},{68,28},{72,3... | collective-permute-start | bytes 786440 | tf_op jit(solution)/shard_map/ppermute | solution.py:25
  360.5 49.9 %collective-permute-start.28 = (bf16[2,128,512]{2,1,0:T(8,128)(2,1)S(1)}, bf16[2,128,512]{2,1,0:T(8,128)(2,1)S(1)}, u32[]{:S(2)}, u32[]{:S(2)}) collective-permute-start(bf16[2,128,512]{2,1,0:T(8,128)(2,1)S(1)} %pad_maximum_fusion.4), channel_id=1, source_target_pairs={{44,0},{48,4},{52,8},{56,12},{60,16},{64,20},{68,24},{72,28},{76,3... | collective-permute-start | bytes 786440 | tf_op jit(solution)/shard_map/ppermute | solution.py:25
  509.9 33.7 %collective-permute-start.33 = (bf16[128,2048]{1,0:T(8,128)(2,1)S(1)}, bf16[128,2048]{1,0:T(8,128)(2,1)S(1)}, u32[]{:S(2)}, u32[]{:S(2)}) collective-permute-start(bf16[128,2048]{1,0:T(8,128)(2,1)S(1)} %collective-permute-done.32), channel_id=1, source_target_pairs={{0,64},{64,0},{4,68},{68,4},{8,72},{72,8},{12,76},{76,12},{16,80},... | collective-permute-start | bytes 1572872 | tf_op jit(solution)/shard_map/ppermute | solution.py:19
  543.6 36.1 %collective-permute-start.34 = (bf16[128,2048]{1,0:T(8,128)(2,1)S(1)}, bf16[128,2048]{1,0:T(8,128)(2,1)S(1)}, u32[]{:S(2)}, u32[]{:S(2)}) collective-permute-start(bf16[128,2048]{1,0:T(8,128)(2,1)S(1)} %collective-permute-done.33), channel_id=1, source_target_pairs={{0,128},{128,0},{4,132},{132,4},{8,136},{136,8},{12,140},{140,12},... | collective-permute-start | bytes 1572872 | tf_op jit(solution)/shard_map/ppermute | solution.py:19
  579.7 56.4 %collective-permute-start.35 = (bf16[128,2048]{1,0:T(8,128)(2,1)S(1)}, bf16[128,2048]{1,0:T(8,128)(2,1)S(1)}, u32[]{:S(2)}, u32[]{:S(2)}) collective-permute-start(bf16[128,2048]{1,0:T(8,128)(2,1)S(1)} %collective-permute-done.34), channel_id=1, source_target_pairs={{0,256},{256,0},{4,260},{260,4},{8,264},{264,8},{12,268},{268,12},... | collective-permute-start | bytes 1572872 | tf_op jit(solution)/shard_map/ppermute | solution.py:19
  (25 other events, 415.3 us)
